TPU v7x, 128 devices: a whole 4x4x4 slice. The times are simulated.
128 devices in a mesh: lon: 8 (over x_lo, y), lat: 16 (over z, x_hi, core).
Axes of the slice: x: 4 (x_hi: 2, x_lo: 2; x = x_hi * 2 + x_lo), y: 4, z: 4, core: 2. Of those that a mesh axis runs over, the one named last changes fastest.
Arguments:
- u_velocity: float32 [16, 2048, 4096], P(None, 'lat', 'lon'), may hold values from -6 to 6
- v_velocity: float32 [16, 2048, 4096], P(None, 'lat', 'lon'), may hold values from -6 to 6
- bottom_level: int32 [2048, 4096], P('lat', 'lon'), may hold values from 0 to 16
- zonal_scale: float32 [2048], P('lat'), may hold values from 0.5 to 2
- mixing: float32 [15], replicated, may hold values from 0.1 to 3
- brick_owner: int32 [128], replicated, may hold values from 0 to 127, each once
Outputs:
- bricks: bfloat16 [128, 128, 4, 16, 128], P(('lon', 'lat'))
Inputs may be any that keep to these rules, and one draw needn't show every extreme that they name: `brick_owner`: a permutation of the device numbers 0 to 127.
All inputs are finite; a program needn't handle non-finite values.
Results may differ from a plain program's by a relative error of at most 0.001.
Values may be sent and summed in bfloat16 or wider, within the bound.
A program may use at most 128 MiB of HBM per device.

v0:
```python
import jax
import jax.numpy as jnp
from jax import lax
from jax.sharding import PartitionSpec as P


def with_halo(cells, sides, width, closed):
    for axis, dim in sides:
        count = lax.axis_size(axis)
        ends = count if closed else count - 1
        head = lax.slice_in_dim(cells, 0, width, axis=dim)
        tail = lax.slice_in_dim(cells, cells.shape[dim] - width, cells.shape[dim], axis=dim)
        cells = jnp.concatenate(
            [
                lax.ppermute(tail, axis, [(i, (i + 1) % count) for i in range(ends)]),
                cells,
                lax.ppermute(head, axis, [((i + 1) % count, i) for i in range(ends)]),
            ],
            axis=dim,
        )
    return cells


def partner_2(shard, axis, stride):
    return lax.ppermute(shard, axis, [(i, i ^ 1 << stride) for i in range(lax.axis_size(axis))])


def fourth(first, second, third, fourth_term):
    return (first - 8.0 * second + 8.0 * third - fourth_term) * (1.0 / 12.0)


def okubo_weiss(zonal_u, zonal_v, north_u, north_v, scale, sea_mask):
    row_scale = scale[:, None]
    du_dx = (
        fourth(zonal_u[..., :-4], zonal_u[..., 1:-3], zonal_u[..., 3:-1], zonal_u[..., 4:])
        * row_scale
    )
    dv_dx = (
        fourth(zonal_v[..., :-4], zonal_v[..., 1:-3], zonal_v[..., 3:-1], zonal_v[..., 4:])
        * row_scale
    )
    du_dy = fourth(
        north_u[..., :-4, :], north_u[..., 1:-3, :], north_u[..., 3:-1, :], north_u[..., 4:, :]
    )
    dv_dy = fourth(
        north_v[..., :-4, :], north_v[..., 1:-3, :], north_v[..., 3:-1, :], north_v[..., 4:, :]
    )
    strain_normal = du_dx - dv_dy
    strain_shear = dv_dx + du_dy
    vorticity = dv_dx - du_dy
    return sea_mask * (
        strain_normal * strain_normal + strain_shear * strain_shear - vorticity * vorticity
    )


def smooth(field, mixing):
    levels = field.shape[0]
    subdiag = [None] + [-mixing[k - 1] for k in range(1, levels)]
    superdiag = [-mixing[k] for k in range(levels - 1)] + [None]
    diagonal = []
    for k in range(levels):
        center = jnp.float32(1.0)
        if k > 0:
            center = center + mixing[k - 1]
        if k < levels - 1:
            center = center + mixing[k]
        diagonal.append(center)
    ratios = []
    forward = []
    for k in range(levels):
        if k == 0:
            divisor = diagonal[0]
            current = field[0] / divisor
        else:
            divisor = diagonal[k] - subdiag[k] * ratios[k - 1]
            current = (field[k] - subdiag[k] * forward[k - 1]) / divisor
        ratios.append(superdiag[k] / divisor if k < levels - 1 else None)
        forward.append(current)
    result = [None] * levels
    result[levels - 1] = forward[levels - 1]
    for k in range(levels - 2, -1, -1):
        result[k] = forward[k] - ratios[k] * result[k + 1]
    return jnp.stack(result)


def body(u_velocity, v_velocity, bottom_level, zonal_scale, mixing, brick_owner):
    levels = u_velocity.shape[0]
    tile_rows = u_velocity.shape[1]
    tile_cols = u_velocity.shape[2]
    sea_mask = (jnp.arange(levels, dtype=jnp.int32)[:, None, None] < bottom_level[None]).astype(
        jnp.float32
    )
    velocity = jnp.stack([u_velocity * sea_mask, v_velocity * sea_mask])
    zonal = with_halo(velocity, (("lon", 3),), 2, True)
    northward = with_halo(velocity, (("lat", 2),), 2, False)
    top_rows = velocity[:, :, tile_rows - 2 :, :]
    bit_count = lax.axis_size("lon").bit_length() - 1
    bit_order = list(range(bit_count))
    partner = top_rows
    for place in bit_order:
        partner = partner_2(partner.astype(jnp.bfloat16), "lon", place).astype(partner.dtype)
    partner = partner[..., ::-1]
    ghost = -partner[:, :, ::-1, :]
    at_top = lax.axis_index("lat") == lax.axis_size("lat") - 1
    upper_rim = jnp.where(at_top, ghost, northward[:, :, tile_rows + 2 :, :])
    northward = jnp.concatenate([northward[:, :, : tile_rows + 2, :], upper_rim], axis=2)
    okubo = okubo_weiss(zonal[0], zonal[1], northward[0], northward[1], zonal_scale, sea_mask)
    smoothed = smooth(okubo, mixing).astype(jnp.bfloat16)
    devices = brick_owner.shape[0]
    row_groups = devices // 16
    lev_brick = levels // 4
    row_brick = tile_rows // row_groups
    col_brick = tile_cols // 4
    pieces = smoothed.reshape(4, lev_brick, row_groups, row_brick, 4, col_brick)
    pieces = jnp.transpose(pieces, (0, 2, 4, 1, 3, 5)).reshape(
        devices, lev_brick, row_brick, col_brick
    )
    slots = jnp.arange(devices, dtype=jnp.int32)
    inverse = jnp.sum(jnp.where(brick_owner[None, :] == slots[:, None], slots[None, :], 0), axis=1)
    outgoing = jnp.take(pieces, inverse, axis=0)
    incoming = lax.all_to_all(outgoing, ("lon", "lat"), split_axis=0, concat_axis=0, tiled=True)
    return incoming[None]


def solution(mesh):
    placed = (P(None, "lat", "lon"), P(None, "lat", "lon"), P("lat", "lon"), P("lat"), P(), P())
    return jax.shard_map(
        body,
        mesh=mesh,
        in_specs=placed,
        out_specs=P(("lon", "lat"), None, None, None, None),
        check_vma=False,
    )
```

profile of v0, /device:TPU:1, one launch (start us, length us, event | category | flops | bytes accessed | tf_op | source)
XLA Modules:
  0.0 169.6 jit_solution(17089687366521856882)
XLA Ops:
  0.0 4.6 %select_bitcast_fusion.1 = (f32[1,16,128,512]{3,2,1,0:T(8,128)S(1)}, f32[1,16,128,512]{3,2,1,0:T(8,128)S(1)}) fusion(f32[16,128,512]{2,1,0:T(8,128)} %param.6, s32[128,512]{1,0:T(8,128)} %param.8, f32[16,128,512]{2,1,0:T(8,128)} %param.7), kind=kLoop, calls=%fused_computation.43 | loop fusion | flops 3145728 | bytes 17039360 | tf_op jit(solution)/shard_map/stack | solution.py:93
  4.7 0.1 fusion.44
  4.8 2.2 %collective-permute-start.3 = (bf16[2,16,2,512]{3,1,2,0:T(8,128)(2,1)S(1)}, bf16[2,16,2,512]{3,1,2,0:T(8,128)(2,1)S(1)}, u32[]{:S(2)}, u32[]{:S(2)}) collective-permute-start(bf16[2,16,2,512]{3,1,2,0:T(8,128)(2,1)S(1)} %copy.40), channel_id=1, source_target_pairs={{0,16},{16,0},{32,48},{48,32},{64,80},{80,64},{96,112},{112,96},{1... | collective-permute-start | bytes 196616 | tf_op jit(solution)/shard_map/ppermute | solution.py:25
  7.0 2.9 %collective-permute-start.6 = (f32[2,16,2,512]{3,1,2,0:T(8,128)S(1)}, f32[2,16,2,512]{3,1,2,0:T(8,128)S(1)}, u32[]{:S(2)}, u32[]{:S(2)}) collective-permute-start(f32[2,16,2,512]{3,1,2,0:T(8,128)S(1)} %copy.42), channel_id=1, source_target_pairs={{1,0},{2,1},{3,2},{4,3},{5,4},{6,5},{7,6},{8,7},{9,8},{10,9},{11,1... | collective-permute-start | bytes 393224 | tf_op jit(solution)/shard_map/ppermute | solution.py:17
  10.0 4.5 %collective-permute-start.2 = (f32[2,16,2,512]{3,1,2,0:T(8,128)S(1)}, f32[2,16,2,512]{3,1,2,0:T(8,128)S(1)}, u32[]{:S(2)}, u32[]{:S(2)}) collective-permute-start(f32[2,16,2,512]{3,1,2,0:T(8,128)S(1)} %copy.39), channel_id=1, source_target_pairs={{0,1},{1,2},{2,3},{3,4},{4,5},{5,6},{6,7},{7,8},{8,9},{9,10},{10,1... | collective-permute-start | bytes 393224 | tf_op jit(solution)/shard_map/ppermute | solution.py:15
  14.5 2.1 %fusion.17 = (f32[2,16,128,2]{3,2,1,0:T(8,128)S(1)}, f32[2,16,128,2]{3,2,1,0:T(8,128)}) fusion(f32[1,16,128,512]{3,2,1,0:T(8,128)S(1)} %get-tuple-element.29, f32[1,16,128,512]{3,2,1,0:T(8,128)S(1)} %get-tuple-element.30), kind=kLoop, calls=%fused_computation.45 | loop fusion | flops 16384 | bytes 8454144 | tf_op jit(solution)/shard_map/stack | solution.py:93
  16.7 2.2 %copy.36 = f32[2,16,128,2]{2,1,3,0:T(8,128)S(1)} copy(f32[2,16,128,2]{3,2,1,0:T(8,128)} %get-tuple-element.27) | data formatting | bytes 65536 | tf_op jit(solution)/shard_map/slice | solution.py:11
  18.9 2.5 %collective-permute-start.1 = (f32[2,16,128,2]{2,1,3,0:T(8,128)S(1)}, f32[2,16,128,2]{2,1,3,0:T(8,128)S(1)}, u32[]{:S(2)}, u32[]{:S(2)}) collective-permute-start(f32[2,16,128,2]{2,1,3,0:T(8,128)S(1)} %copy.36), channel_id=1, source_target_pairs={{16,0},{32,16},{48,32},{64,48},{80,64},{96,80},{112,96},{0,112},{1... | collective-permute-start | bytes 98312 | tf_op jit(solution)/shard_map/ppermute | solution.py:17
  21.4 0.6 copy.35
  22.1 0.0 collective-permute-start
  22.1 0.1 select_reduce_fusion
  22.3 0.7 fusion.46
  51.6 0.0 collective-permute-done
  51.6 0.6 copy.37
  52.2 2.0 %copy.38 = f32[2,16,128,2]{3,2,1,0:T(8,128)} copy(f32[2,16,128,2]{2,1,3,0:T(8,128)S(1)} %collective-permute-done.1) | data formatting | bytes 65536 | tf_op jit(solution)/shard_map/ppermute | solution.py:17
  54.2 1.6 collective-permute-start.4
  55.8 11.3 %pad_maximum_fusion = f32[2,16,128,516]{3,2,1,0:T(8,128)} fusion(f32[2,16,128,2]{3,2,1,0:T(8,128)} %copy.38, f32[1,16,128,512]{3,2,1,0:T(8,128)} %copy-done.1, f32[1,16,128,512]{3,2,1,0:T(8,128)} %copy-done, f32[2,16,128,2]{3,2,1,0:T(8,128)S(1)} %copy.37), kind=kLoop, calls=%fused_computation.7 | loop fusion | flops 6340608 | bytes 16908288 | tf_op jit(solution)/shard_map/concatenate | solution.py:13
  67.1 0.9 collective-permute-start.5
  68.0 9.1 %slice_bitcast_fusion = (f32[16,128,516]{2,1,0:T(8,128)}, f32[16,128,516]{2,1,0:T(8,128)}) fusion(f32[2,16,128,516]{3,2,1,0:T(8,128)} %pad_maximum_fusion), kind=kLoop, calls=%fused_computation.9 | loop fusion | bytes 16908288 | tf_op jit(solution)/shard_map/squeeze | solution.py:107
  77.1 0.1 copy.44
  77.2 0.1 copy_convert_fusion
  77.3 0.8 rev.4
  78.1 0.1 copy_select_fusion
  78.3 6.7 %pad_maximum_fusion.1 = f32[2,16,132,512]{3,2,1,0:T(8,128)} fusion(f32[2,16,2,512]{3,2,1,0:T(2,128)S(1)} %copy_select_fusion, f32[1,16,128,512]{3,2,1,0:T(8,128)} %copy-done.1, f32[1,16,128,512]{3,2,1,0:T(8,128)} %copy-done, f32[2,16,2,512]{3,2,1,0:T(2,128)S(1)} %copy.44), kind=kLoop, calls=%fused_computation.8 | loop fusion | flops 6488064 | bytes 17301504 | tf_op jit(solution)/shard_map/concatenate | solution.py:106
  85.0 4.8 %slice_bitcast_fusion.2 = (f32[16,132,512]{2,1,0:T(8,128)S(1)}, f32[16,132,512]{2,1,0:T(8,128)S(1)}) fusion(f32[2,16,132,512]{3,2,1,0:T(8,128)} %pad_maximum_fusion.1), kind=kLoop, calls=%fused_computation.11 | loop fusion | bytes 17301504 | tf_op jit(solution)/shard_map/squeeze | solution.py:107
  89.8 15.5 %fusion.11 = f32[16,128,512]{2,1,0:T(8,128)} fusion(f32[16,132,512]{2,1,0:T(8,128)S(1)} %get-tuple-element.25, f32[16,128,516]{2,1,0:T(8,128)} %get-tuple-element.23, f32[16,128,516]{2,1,0:T(8,128)S(1)} %bitcast.36, f32[16,132,512]{2,1,0:T(8,128)S(1)} %get-tuple-element.24, f32[128]{0:T(128)S(1)} %broadcast_multiply_fusion, s32[128,512]{1,0:T(8,128)S(1)} %copy-done.2), kind=kLoop, calls=%fused_computation.31 | loop fusion | flops 35651584 | bytes 71565824 | tf_op jit(solution)/shard_map/mul | solution.py:51
  105.4 3.7 %fusion.35 = (bf16[16,128,512]{2,1,0:T(8,128)(2,1)}, bf16[1,128,512]{2,1,0:T(8,128)(2,1)S(1)}, f32[1,128,512]{2,1,0:T(8,128)S(1)}, f32[1,128,512]{2,1,0:T(8,128)...) fusion(f32[]{:T(128)S(6)} %div.399, f32[]{:T(128)} %bitcast.6, ...), kind=kLoop, calls=%fused_computation.95 | loop fusion | flops 5111807 | bytes 7864504
  109.0 0.7 convert_dynamic-update-slice_fusion.14
  109.7 0.7 convert_dynamic-update-slice_fusion.13
  110.4 0.7 convert_dynamic-update-slice_fusion.12
  111.0 0.7 convert_dynamic-update-slice_fusion.11
  111.7 0.7 convert_dynamic-update-slice_fusion.10
  112.4 0.7 convert_dynamic-update-slice_fusion.9
  113.1 0.7 convert_dynamic-update-slice_fusion.8
  113.8 0.7 convert_dynamic-update-slice_fusion.7
  114.5 0.7 convert_dynamic-update-slice_fusion.6
  115.1 0.7 convert_dynamic-update-slice_fusion.5
  115.8 0.7 convert_dynamic-update-slice_fusion.4
  116.5 0.7 convert_dynamic-update-slice_fusion.3
  117.2 0.7 convert_dynamic-update-slice_fusion.2
  117.9 1.7 convert_dynamic-update-slice_fusion.1
  119.5 1.7 convert_dynamic-update-slice_fusion
  121.2 2.5 %convert_element_type.18 = bf16[4,4,8,16,4,128]{5,4,3,2,1,0:T(4,128)(2,1)S(1)} reshape(bf16[16,128,512]{2,1,0:T(8,128)(2,1)} %convert_dynamic-update-slice_fusion) | data formatting | bytes 4194304 | tf_op jit(solution)/shard_map/convert_element_type | solution.py:108
  123.7 1.9 %copy.45 = bf16[4,8,4,4,16,128]{5,4,3,2,1,0:T(8,128)(2,1)} copy(bf16[4,8,4,4,16,128]{5,2,4,1,3,0:T(4,128)(2,1)S(1)} %bitcast.38) | data formatting | bytes 4194304 | tf_op jit(solution)/shard_map/transpose | solution.py:115
  125.6 2.5 %gather_fusion = bf16[128,4,16,128]{3,2,1,0:T(8,128)(2,1)S(1)} fusion(bf16[128,4,16,128]{3,2,1,0:T(8,128)(2,1)} %bitcast.37, s32[1024]{0:T(1024)S(1)} %pad_clamp_fusion), kind=kCustom, calls=%fused_computation | custom fusion | bytes 4194816 | tf_op jit(solution)/shard_map/jit(_take)/gather | solution.py:120
  128.2 0.3 broadcast_select_fusion
  128.5 39.8 %all_to_all.5 = bf16[128,4,16,128]{3,2,1,0:T(8,128)(2,1)S(1)} all-to-all(bf16[128,4,16,128]{3,2,1,0:T(8,128)(2,1)S(1)} %broadcast_select_fusion), channel_id=1, replica_groups=mesh['lon'=8,'lat'=16] {'lon','lat'}, dimensions={0} | all-to-all | bytes 4194304 | tf_op jit(solution)/shard_map/all_to_all | solution.py:121
  168.3 1.3 copy.64
  (30 shorter events, 0.1 us)
Async XLA Ops:
  4.6 9.9 %copy-start = (f32[1,16,128,512]{3,2,1,0:T(8,128)}, f32[1,16,128,512]{3,2,1,0:T(8,128)S(1)}, u32[]{:S(2)}) copy-start(f32[1,16,128,512]{3,2,1,0:T(8,128)S(1)} %get-tuple-element.29) | copy-start | bytes 12582916
  4.7 9.9 %copy-start.1 = (f32[1,16,128,512]{3,2,1,0:T(8,128)}, f32[1,16,128,512]{3,2,1,0:T(8,128)S(1)}, u32[]{:S(2)}) copy-start(f32[1,16,128,512]{3,2,1,0:T(8,128)S(1)} %get-tuple-element.30) | copy-start | bytes 12582916
  4.8 49.4 %collective-permute-start.3 = (bf16[2,16,2,512]{3,1,2,0:T(8,128)(2,1)S(1)}, bf16[2,16,2,512]{3,1,2,0:T(8,128)(2,1)S(1)}, u32[]{:S(2)}, u32[]{:S(2)}) collective-permute-start(bf16[2,16,2,512]{3,1,2,0:T(8,128)(2,1)S(1)} %copy.40), channel_id=1, source_target_pairs={{0,16},{16,0},{32,48},{48,32},{64,80},{80,64},{96,112},{112,96},{1... | collective-permute-start | bytes 196616 | tf_op jit(solution)/shard_map/ppermute | solution.py:25
  7.0 71.1 %collective-permute-start.6 = (f32[2,16,2,512]{3,1,2,0:T(8,128)S(1)}, f32[2,16,2,512]{3,1,2,0:T(8,128)S(1)}, u32[]{:S(2)}, u32[]{:S(2)}) collective-permute-start(f32[2,16,2,512]{3,1,2,0:T(8,128)S(1)} %copy.42), channel_id=1, source_target_pairs={{1,0},{2,1},{3,2},{4,3},{5,4},{6,5},{7,6},{8,7},{9,8},{10,9},{11,1... | collective-permute-start | bytes 393224 | tf_op jit(solution)/shard_map/ppermute | solution.py:17
  10.0 67.2 %collective-permute-start.2 = (f32[2,16,2,512]{3,1,2,0:T(8,128)S(1)}, f32[2,16,2,512]{3,1,2,0:T(8,128)S(1)}, u32[]{:S(2)}, u32[]{:S(2)}) collective-permute-start(f32[2,16,2,512]{3,1,2,0:T(8,128)S(1)} %copy.39), channel_id=1, source_target_pairs={{0,1},{1,2},{2,3},{3,4},{4,5},{5,6},{6,7},{7,8},{8,9},{9,10},{10,1... | collective-permute-start | bytes 393224 | tf_op jit(solution)/shard_map/ppermute | solution.py:15
  16.7 5.4 %copy-start.4 = (s32[128]{0:T(128)S(1)}, s32[128]{0:T(128)}, u32[]{:S(2)}) copy-start(s32[128]{0:T(128)} %param.11) | copy-start | bytes 1540
  16.7 5.6 %copy-start.5 = (f32[128]{0:T(128)S(1)}, f32[128]{0:T(128)}, u32[]{:S(2)}) copy-start(f32[128]{0:T(128)} %param.9) | copy-start | bytes 1540
  16.7 5.6 %copy-start.3 = (f32[15]{0:T(128)S(1)}, f32[15]{0:T(128)}, u32[]{:S(2)}) copy-start(f32[15]{0:T(128)} %param.10) | copy-start | bytes 184
  18.9 33.3 %collective-permute-start.1 = (f32[2,16,128,2]{2,1,3,0:T(8,128)S(1)}, f32[2,16,128,2]{2,1,3,0:T(8,128)S(1)}, u32[]{:S(2)}, u32[]{:S(2)}) collective-permute-start(f32[2,16,128,2]{2,1,3,0:T(8,128)S(1)} %copy.36), channel_id=1, source_target_pairs={{16,0},{32,16},{48,32},{64,48},{80,64},{96,80},{112,96},{0,112},{1... | collective-permute-start | bytes 98312 | tf_op jit(solution)/shard_map/ppermute | solution.py:17
  22.1 29.5 %collective-permute-start = (f32[2,16,128,2]{2,1,3,0:T(8,128)S(1)}, f32[2,16,128,2]{2,1,3,0:T(8,128)S(1)}, u32[]{:S(2)}, u32[]{:S(2)}) collective-permute-start(f32[2,16,128,2]{2,1,3,0:T(8,128)S(1)} %copy.35), channel_id=1, source_target_pairs={{0,16},{16,32},{32,48},{48,64},{64,80},{80,96},{96,112},{112,0},{1... | collective-permute-start | bytes 98312 | tf_op jit(solution)/shard_map/ppermute | solution.py:15
  54.2 12.9 %collective-permute-start.4 = (bf16[2,16,2,512]{3,1,2,0:T(8,128)(2,1)S(1)}, bf16[2,16,2,512]{3,1,2,0:T(8,128)(2,1)S(1)}, u32[]{:S(2)}, u32[]{:S(2)}) collective-permute-start(bf16[2,16,2,512]{3,1,2,0:T(8,128)(2,1)S(1)} %collective-permute-done.3), channel_id=1, source_target_pairs={{0,32},{16,48},{32,0},{48,16},{64,96},{80,112},{96,64},{112,80},{1... | collective-permute-start | bytes 196616 | tf_op jit(solution)/shard_map/ppermute | solution.py:25
  67.1 10.1 %collective-permute-start.5 = (bf16[2,16,2,512]{3,1,2,0:T(8,128)(2,1)S(1)}, bf16[2,16,2,512]{3,1,2,0:T(8,128)(2,1)S(1)}, u32[]{:S(2)}, u32[]{:S(2)}) collective-permute-start(bf16[2,16,2,512]{3,1,2,0:T(8,128)(2,1)S(1)} %collective-permute-done.4), channel_id=1, source_target_pairs={{0,64},{16,80},{32,96},{48,112},{64,0},{80,16},{96,32},{112,48},{1... | collective-permute-start | bytes 196616 | tf_op jit(solution)/shard_map/ppermute | solution.py:25
  78.3 11.5 %slice-start = ((s8[5242880]{0:T(1024)(128)(4,1)}), s8[4194304]{0:T(1024)(128)(4,1)S(1)}, s32[]{:S(2)}) async-start(s8[5242880]{0:T(1024)(128)(4,1)} %bitcast.35), calls=%async_computation.1 | async-start | bytes 8388608
  85.0 4.8 %slice-start.1 = ((s8[5242880]{0:T(1024)(128)(4,1)}), s8[1048576]{0:T(1024)(128)(4,1)S(1)}, s32[]{:S(2)}) async-start(s8[5242880]{0:T(1024)(128)(4,1)} %bitcast.35), calls=%async_computation.2 | async-start | bytes 2097152
  85.0 4.8 %copy-start.2 = (s32[128,512]{1,0:T(8,128)S(1)}, s32[128,512]{1,0:T(8,128)}, u32[]{:S(2)}) copy-start(s32[128,512]{1,0:T(8,128)} %param.8) | copy-start | bytes 786436
where the time goes:
time: 170 us
  other arithmetic  56.2 us (33%)
  blocking collectives  39.8 us (23%)
  local copies, waits for them, and re-layouts  30.1 us (18%)
  between operations  28.9 us (17%)
  starting transfers between devices  14.6 us (9%)
    all_to_all x1, blocking collectives, body(): lax.all_to_all(outgoing, ('lon', 'lat'), split_axis=0, concat_axis=0, til...  39.8 us
    mul x1, other arithmetic, okubo_weiss(): sea_mask * (strain_normal * strain_normal + strain_shear * strain_shear -...  15.5 us
    unnamed x15, other arithmetic  13.5 us
    concatenate x1, other arithmetic, with_halo(): jnp.concatenate([lax.ppermute(tail, axis, [(i, (i + 1) % count) for i in...  11.3 us
    squeeze x1, local copies, waits for them, and re-layouts, body(): zonal[1]  9.12 us
    another operation x2, other arithmetic, body(): velocity = jnp.stack([u_velocity * sea_mask, v_velocity * sea_mask])  6.78 us
    concatenate x1, other arithmetic, body(): jnp.concatenate([northward[:, :, :tile_rows + 2, :], upper_rim], axis=2)  6.66 us
    ppermute x2, starting transfers between devices, with_halo(): lax.ppermute(head, axis, [((i + 1) % count, i) for i in range(ends)])  5.38 us
  transfers between devices with their start and end apart: 7, of which 0 were waited for; matrix products, arithmetic and copies ran while one was open for 18% of the time, Pallas kernels for 0%

commit v1 on v0

v1 whole, which is shorter than its diff:
```python
import jax
import jax.numpy as jnp
from jax import lax
from jax.experimental import pallas as pl
from jax.experimental.pallas import tpu as pltpu
from jax.sharding import PartitionSpec as P

MESH = pl.DeviceIdType.MESH
LEV, ROWS, TILES, LANES = 16, 128, 4, 128
N_LON, N_LAT = 8, 16
DEVICES = N_LON * N_LAT
COLUMNS = 32
GROUP = 4


def target(lon, lat, step):
    off = (step * 101) % DEVICES
    x = (lat % 4 // 2 * 2 + lon // 4 + off % 4) % 4
    y = (lon % 4 + off // 4 % 4) % 4
    z = (lat // 4 + off // 16 % 4) % 4
    core = (lat % 2 + off // 64) % 2
    return x % 2 * 4 + y, z * 4 + x // 2 * 2 + core


def plan(brick_owner):
    lon, lat = lax.axis_index("lon"), lax.axis_index("lat")
    steps = jnp.arange(DEVICES, dtype=jnp.int32)
    to_lon, to_lat = target(lon, lat, steps + 1)
    dest = to_lon * N_LAT + to_lat
    place = jnp.sum(jnp.where(brick_owner[None, :] == dest[:, None], steps[None, :], 0), axis=1)
    return place


def kernel(
    u_hbm, v_hbm, bottom_hbm, scale_ref, mixing_ref, plan_ref, out_ref,
    ub, vb, bottom, scale, coef, bricks, outbox, rows_out, rows_in, cols_out, cols_in,
    load_sem, bottom_sem, halo_send, halo_recv, own_sem, send_sem, recv_sem, ready,
):
    lon, lat = lax.axis_index("lon"), lax.axis_index("lat")
    me = lon * N_LAT + lat
    barrier = pltpu.get_barrier_semaphore()

    def signal(sem, to):
        pl.semaphore_signal(sem, inc=1, device_id=to, device_id_type=MESH)

    for k in range(1, N_LAT):
        signal(barrier, (lon, (lat + k) % N_LAT))
    for k in range(1, N_LON):
        signal(barrier, ((lon + k) % N_LON, lat))

    loads = []
    for t in range(TILES):
        cut = pl.ds(t * LANES, LANES)
        c = pltpu.make_async_copy(bottom_hbm.at[:, cut], bottom.at[t], bottom_sem.at[t])
        c.start()
        loads.append(c)
    for g in range(LEV // GROUP):
        for t in range(TILES):
            cut = pl.ds(t * LANES, LANES)
            levels = pl.ds(g * GROUP, GROUP)
            for f, (src, dst) in enumerate(((u_hbm, ub), (v_hbm, vb))):
                c = pltpu.make_async_copy(
                    src.at[levels, :, cut],
                    dst.at[levels, t + 1, pl.ds(8, ROWS), :],
                    load_sem.at[g, t, f],
                )
                c.start()
                loads.append(c)

    scale[...] = jnp.broadcast_to(scale_ref[...], (ROWS, LANES)).T
    one = jnp.ones((8, LANES), jnp.float32)
    ratio = None
    for k in range(LEV):
        above = mixing_ref[k - 1] * one if k > 0 else None
        below = mixing_ref[k] * one if k < LEV - 1 else None
        pivot = one
        if k > 0:
            pivot = pivot + above
        if k < LEV - 1:
            pivot = pivot + below
        if k > 0:
            pivot = pivot - above * ratio
        inverse = 1.0 / pivot
        coef[k] = inverse * (1.0 / 144.0)
        if k > 0:
            coef[LEV + k] = above * inverse
        if k < LEV - 1:
            ratio = below * inverse
            coef[2 * LEV + k] = ratio

    sub = lax.broadcasted_iota(jnp.int32, (8, LANES), 0)
    lane = lax.broadcasted_iota(jnp.int32, (64, LANES), 1)

    for c in loads[:TILES]:
        c.wait()
    west = jnp.zeros((64, LANES), jnp.float32)
    east = jnp.zeros((64, LANES), jnp.float32)
    for g in range(LEV // GROUP):
        for c in loads[TILES + g * 2 * TILES : TILES + (g + 1) * 2 * TILES]:
            c.wait()

        def mask_pair(n, carry):
            west, east = carry
            for j in range(2):
                k = g * GROUP + 2 * n + j
                for t in range(TILES):
                    sea = bottom[t] > k
                    for buf in (ub, vb):
                        now = buf[k, t + 1, pl.ds(8, ROWS), :]
                        buf[k, t + 1, pl.ds(8, ROWS), :] = jnp.where(sea, now, 0.0)
                for f, buf in enumerate((ub, vb)):
                    at = 4 * k + 2 * f
                    for half in range(2):
                        first = buf[k, 1, pl.ds(8 + 64 * half, 64), :]
                        last = buf[k, TILES, pl.ds(8 + 64 * half, 64), :]
                        spot = at + 64 * half
                        here = (lane >= spot) & (lane < spot + 2)
                        west = jnp.where(here, pltpu.roll(first, spot, 1), west)
                        east = jnp.where(here, pltpu.roll(last, (spot + 2) % LANES, 1), east)
            k = g * GROUP + 2 * n
            pair = k // 2
            for t in range(TILES):
                top = [b[k + j, t + 1, pl.ds(ROWS, 8), :] for j in range(2) for b in (ub, vb)]
                low = [b[k + j, t + 1, pl.ds(8, 8), :] for j in range(2) for b in (ub, vb)]
                top = [pltpu.roll(x, s, 0) if s else x for x, s in zip(top, (2, 4, 6, 0))]
                low = [pltpu.roll(x, s, 0) if s else x for x, s in zip(low, (0, 2, 4, 6))]
                for side, q in ((0, top), (1, low)):
                    rows_out[side, pair, t] = jnp.where(
                        sub < 4, jnp.where(sub < 2, q[0], q[1]), jnp.where(sub < 6, q[2], q[3])
                    )
            return west, east

        west, east = lax.fori_loop(0, GROUP // 2, mask_pair, (west, east))
    cols_out[0] = west
    cols_out[1] = east

    pl.semaphore_wait(barrier, N_LAT - 1 + N_LON - 1)
    for k in range(1, N_LON):
        signal(ready, ((lon + k) % N_LON, lat))

    def column_copy(side):
        to = (lon + (N_LON - 1 if side == 0 else 1)) % N_LON
        return pltpu.make_async_remote_copy(
            cols_out.at[side], cols_in.at[side], halo_send.at[side], halo_recv.at[side],
            device_id=(to, lat), device_id_type=MESH,
        )

    def row_copy(src, dst, sem, to):
        return pltpu.make_async_remote_copy(
            rows_out.at[src], rows_in.at[dst], halo_send.at[sem], halo_recv.at[2 + dst],
            device_id=to, device_id_type=MESH,
        )

    top_tile = lat == N_LAT - 1
    north = row_copy(0, 0, 2, (lon, (lat + 1) % N_LAT))
    fold = row_copy(0, 1, 2, (N_LON - 1 - lon, lat))
    south = row_copy(1, 1, 3, (lon, (lat + N_LAT - 1) % N_LAT))

    @pl.when(top_tile)
    def _():
        fold.start()

    @pl.when(jnp.logical_not(top_tile))
    def _():
        north.start()

    @pl.when(lat > 0)
    def _():
        south.start()

    for side in range(2):
        column_copy(side).start()

    @pl.when(lat == 0)
    def _():
        rows_in[0] = jnp.zeros(rows_in.shape[1:], jnp.float32)

    for side in range(2):
        column_copy(side).wait_recv()

    def spread_columns(k, _):
        for f, buf in enumerate((ub, vb)):
            for half in range(2):
                spot = 4 * k + 2 * f + 64 * half
                rows = pl.ds(8 + 64 * half, 64)
                buf[k, 0, rows, :] = pltpu.roll(cols_in[1], (126 - spot + LANES) % LANES, 1)
                buf[k, TILES + 1, rows, :] = pltpu.roll(cols_in[0], (LANES - spot) % LANES, 1)
        return _

    lax.fori_loop(0, LEV, spread_columns, 0)

    @pl.when(lat > 0)
    def _():
        north.wait_recv()

    south.wait_recv()

    @pl.when(top_tile)
    def _():
        lanes = lax.broadcasted_iota(jnp.int32, (8, LANES), 1)

        def turn(pair, _):
            old = [rows_in[1, pair, t] for t in range(TILES)]
            for t in range(TILES):
                x = old[TILES - 1 - t]
                x = jnp.where(sub % 2 == 0, pltpu.roll(x, 7, 0), pltpu.roll(x, 1, 0))
                rows_in[1, pair, t] = -jnp.take_along_axis(x, LANES - 1 - lanes, axis=1)
            return _

        lax.fori_loop(0, LEV // 2, turn, 0)

    def spread_rows(pair, _):
        for t in range(TILES):
            for side, shifts, rows in ((0, (6, 4, 2, 0), pl.ds(0, 8)), (1, (0, 6, 4, 2), pl.ds(ROWS + 8, 8))):
                x = rows_in[side, pair, t]
                for n, s in enumerate(shifts):
                    buf = (ub, vb)[n % 2]
                    buf[2 * pair + n // 2, t + 1, rows, :] = pltpu.roll(x, s, 0) if s else x
        return _

    lax.fori_loop(0, LEV // 2, spread_rows, 0)

    lanes = lax.broadcasted_iota(jnp.int32, (8, LANES), 1)

    def slopes(buf, k, c, row):
        here = buf[k, c + 1, pl.ds(row + 8, 8), :]
        left = buf[k, c, pl.ds(row + 8, 8), :]
        right = buf[k, c + 2, pl.ds(row + 8, 8), :]

        def beside(s):
            if s < 0:
                return pltpu.roll(jnp.where(lanes < LANES + s, here, left), -s, 1)
            return pltpu.roll(jnp.where(lanes >= s, here, right), LANES - s, 1)

        def above(s):
            return buf[k, c + 1, pl.ds(row + 8 + s, 8), :]

        def slope(at):
            return (at(-2) - at(2)) + 8.0 * (at(1) - at(-1))

        return slope(beside), slope(above)

    def compute(j):
        c = j % TILES
        row0 = pl.multiple_of(j // TILES * 16, 16)
        halves = []
        for h in range(2):
            row = row0 + 8 * h
            depth = bottom[c, pl.ds(row, 8), :]
            wide = scale[pl.ds(row, 8), :]
            wide4 = 4.0 * wide
            state = []
            for k in range(LEV):
                ux, uy = slopes(ub, k, c, row)
                vx, vy = slopes(vb, k, c, row)
                strain = ux * wide - vy
                okubo = strain * strain + (vx * wide4) * uy
                value = okubo * jnp.where(depth > k, coef[k], 0.0)
                if k > 0:
                    value = value + coef[LEV + k] * state[k - 1]
                state.append(value)
            for k in range(LEV - 2, -1, -1):
                state[k] = state[k] + coef[2 * LEV + k] * state[k + 1]
            halves.append(state)
        for k in range(LEV):
            both = jnp.concatenate([halves[0][k], halves[1][k]], axis=0)
            bricks[k // 4 * COLUMNS + j, k % 4] = both.astype(jnp.bfloat16)

    def send(step):
        to_lon, to_lat = target(lon, lat, step + 1)
        outbox[step] = bricks[plan_ref[step]]
        pltpu.make_async_remote_copy(
            outbox.at[step], out_ref.at[me], send_sem, recv_sem,
            device_id=(to_lon, to_lat), device_id_type=MESH,
        ).start()

    compute(0)
    pl.semaphore_wait(ready, N_LON - 1)

    def more(j, _):
        compute(j)
        return _

    lax.fori_loop(1, COLUMNS, more, 0)

    def rest(step, _):
        send(step)
        return _

    lax.fori_loop(0, DEVICES - 1, rest, 0)
    out_ref[me] = bricks[plan_ref[DEVICES - 1]]

    column_copy(0).wait_send()
    column_copy(1).wait_send()
    north.wait_send()

    @pl.when(lat > 0)
    def _():
        south.wait_send()

    whole = pltpu.make_async_remote_copy(
        outbox.at[pl.ds(0, DEVICES - 1)], out_ref.at[pl.ds(0, DEVICES - 1)], send_sem, recv_sem,
        device_id=(lon, lat), device_id_type=MESH,
    )
    whole.wait_send()
    whole.wait_recv()


def body(u_velocity, v_velocity, bottom_level, zonal_scale, mixing, brick_owner):
    brick = (DEVICES, 4, 16, LANES)
    dma = pltpu.SemaphoreType.DMA
    vmem, smem, hbm = (
        pl.BlockSpec(memory_space=pltpu.VMEM),
        pl.BlockSpec(memory_space=pltpu.SMEM),
        pl.BlockSpec(memory_space=pltpu.HBM),
    )
    out = pl.pallas_call(
        kernel,
        out_shape=pltpu.VMEM(brick, jnp.bfloat16),
        in_specs=[hbm, hbm, hbm, vmem, smem, smem],
        out_specs=vmem,
        scratch_shapes=[
            pltpu.VMEM((LEV, TILES + 2, ROWS + 16, LANES), jnp.float32),
            pltpu.VMEM((LEV, TILES + 2, ROWS + 16, LANES), jnp.float32),
            pltpu.VMEM((TILES, ROWS, LANES), jnp.int32),
            pltpu.VMEM((ROWS, LANES), jnp.float32),
            pltpu.VMEM((3 * LEV, 8, LANES), jnp.float32),
            pltpu.VMEM(brick, jnp.bfloat16),
            pltpu.VMEM(brick, jnp.bfloat16),
            pltpu.VMEM((2, LEV // 2, TILES, 8, LANES), jnp.float32),
            pltpu.VMEM((2, LEV // 2, TILES, 8, LANES), jnp.float32),
            pltpu.VMEM((2, 64, LANES), jnp.float32),
            pltpu.VMEM((2, 64, LANES), jnp.float32),
            dma((LEV // GROUP, TILES, 2)),
            dma((TILES,)),
            dma((4,)),
            dma((4,)),
            dma,
            dma,
            dma,
            pltpu.SemaphoreType.REGULAR,
        ],
        compiler_params=pltpu.CompilerParams(
            collective_id=0, has_side_effects=True, vmem_limit_bytes=48 << 20
        ),
    )(u_velocity, v_velocity, bottom_level, zonal_scale[None], mixing, plan(brick_owner))
    return out[None]


def solution(mesh):
    placed = (P(None, "lat", "lon"), P(None, "lat", "lon"), P("lat", "lon"), P("lat"), P(), P())
    return jax.shard_map(
        body,
        mesh=mesh,
        in_specs=placed,
        out_specs=P(("lon", "lat"), None, None, None, None),
        check_vma=False,
    )
```

time: 170 us -> 61.9 us (0.36)
  Pallas kernels: 0 us -> 57.2 us
  other arithmetic: 56.2 us -> 0.87 us
  blocking collectives: 39.8 us -> 0 us
  between operations: 28.9 us -> 0.03 us
  local copies, waits for them, and re-layouts: 30.1 us -> 3.58 us
  starting transfers between devices: 14.6 us -> 0 us
    pallas_call x0 -> x1, Pallas kernels: none -> 57.2 us  [body(): pl.pallas_call(kernel, out_shape=pltpu.VMEM(brick, jnp.bfloat16), in_spec...]
    all_to_all x1 -> x0, blocking collectives: 39.8 us -> none  [body(): lax.all_to_all(outgoing, ('lon', 'lat'), split_axis=0, concat_axis=0, til...]
    concatenate x2 -> x0, other arithmetic: 18 us -> none  [the longest x1 11.3 us: with_halo(): jnp.concatenate([lax.ppermute(tail, axis, [(i, (i + 1) % count) for i in...]
    mul x2 -> x0, other arithmetic: 15.6 us -> none  [the longest x1 15.5 us: okubo_weiss(): sea_mask * (strain_normal * strain_normal + strain_shear * strain_shear -...]
    ppermute x7 -> x0, starting transfers between devices: 14.6 us -> none  [the longest x2 5.38 us: with_halo(): lax.ppermute(head, axis, [((i + 1) % count, i) for i in range(ends)])]
    squeeze x2 -> x0, local copies, waits for them, and re-layouts: 13.9 us -> none  [the longest x1 9.12 us: body(): zonal[1]]
    unnamed x15 -> x0, other arithmetic: 13.5 us -> none
    another operation x3 -> x0, other arithmetic: 8.43 us -> none  [the longest x2 6.78 us: body(): velocity = jnp.stack([u_velocity * sea_mask, v_velocity * sea_mask])]
  transfers between devices with their start and end apart: 7 -> 0, of which waited for: 0 -> 0; matrix products, arithmetic and copies ran while one was open for 18% -> 0% of each run, Pallas kernels for 0% -> 0%
where the time goes in v1:
time: 61.9 us; the launch traced here: 61.7 us
  Pallas kernels  57.2 us (92%)
  local copies, waits for them, and re-layouts  3.58 us (6%)
  other arithmetic  0.87 us (1%)
    pallas_call x1, Pallas kernels, body(): pl.pallas_call(kernel, out_shape=pltpu.VMEM(brick, jnp.bfloat16), in_spec...  57.2 us
    unnamed x7, local copies, waits for them, and re-layouts  3.58 us

profile of v1, /device:TPU:1, one launch (start us, length us, event | category | flops | bytes accessed | tf_op | source)
XLA Modules:
  0.0 61.7 jit_solution(14851409214428848832)
XLA Ops:
  0.0 0.8 %select_reduce_fusion.plan_ref = s32[128]{0:T(128)S(1)} fusion(s32[128]{0:T(128)} %param.11, s32[128]{0:T(128)S(1)} %fusion.2), kind=kLoop, calls=%fused_computation | loop fusion | flops 49024 | bytes 1536 | tf_op jit(solution)/shard_map/reduce_sum | solution.py:30
  0.9 0.0 copy-start
  0.9 0.9 %copy-done = s32[128,512]{1,0:T(8,128)S(1)} copy-done((s32[128,512]{1,0:T(8,128)S(1)}, s32[128,512]{1,0:T(8,128)}, u32[]{:S(2)}) %copy-start) | copy-done | bytes 262168
  1.8 0.0 copy-start.1
  1.8 0.7 %copy-done.1 = f32[128]{0:T(128)S(1)} copy-done((f32[128]{0:T(128)S(1)}, f32[128]{0:T(128)}, u32[]{:S(2)}) %copy-start.1) | copy-done | bytes 536
  2.5 0.0 copy-start.2
  2.5 0.7 %copy-done.2 = f32[15]{0:T(128)S(1)} copy-done((f32[15]{0:T(128)S(1)}, f32[15]{0:T(128)}, u32[]{:S(2)}) %copy-start.2) | copy-done | bytes 84
  3.1 57.2 %shard_map.64 = bf16[128,4,16,128]{3,2,1,0:T(8,128)(2,1)S(1)} custom-call(f32[16,128,512]{2,1,0:T(8,128)} %u_hbm.1, f32[16,128,512]{2,1,0:T(8,128)} %v_hbm.1, s32[128,512]{1,0:T(8,128)S(1)} %copy-done, f32[1,128]{1,0:T(1,128)S(1)} %bitcast.3, f32[15]{0:T(128)S(1)} %copy-done.2, s32[128]{0:T(128)S(1)} %select_reduce_fusion.plan_ref), custom_call_target="tpu_custom_call" | custom-call | tf_op jit(solution)/shard_map/pallas_call | solution.py:317
  60.4 1.3 %copy.8 = bf16[1,128,4,16,128]{4,3,2,1,0:T(8,128)(2,1)} copy(bf16[1,128,4,16,128]{4,3,2,1,0:T(8,128)(2,1)S(1)} %bitcast.2) | data formatting | bytes 4194304
  (1 shorter events, 0.0 us)
Async XLA Ops:
  0.9 1.0 %copy-start = (s32[128,512]{1,0:T(8,128)S(1)}, s32[128,512]{1,0:T(8,128)}, u32[]{:S(2)}) copy-start(s32[128,512]{1,0:T(8,128)} %bottom_hbm.1) | copy-start | bytes 786436
  1.8 0.7 %copy-start.1 = (f32[128]{0:T(128)S(1)}, f32[128]{0:T(128)}, u32[]{:S(2)}) copy-start(f32[128]{0:T(128)} %param.9) | copy-start | bytes 1540
  2.5 0.7 %copy-start.2 = (f32[15]{0:T(128)S(1)}, f32[15]{0:T(128)}, u32[]{:S(2)}) copy-start(f32[15]{0:T(128)} %mixing_ref.1) | copy-start | bytes 184

commit v2 on v1

--- a/solution.py
+++ b/solution.py
@@ -10,6 +10,7 @@
 N_LON, N_LAT = 8, 16
 DEVICES = N_LON * N_LAT
 COLUMNS = 32
+PARTS = 3
 GROUP = 4
 
 
@@ -28,12 +29,39 @@
     to_lon, to_lat = target(lon, lat, steps + 1)
     dest = to_lon * N_LAT + to_lat
     place = jnp.sum(jnp.where(brick_owner[None, :] == dest[:, None], steps[None, :], 0), axis=1)
-    return place
+    column = place % COLUMNS
+    columns = jnp.arange(COLUMNS, dtype=jnp.int32)
+    hit = column[None, :] == columns[:, None]
+    need = jnp.min(jnp.where(hit, steps[None, :], DEVICES), axis=1)
+    slot = jnp.sum((need[None, :] < need[:, None]).astype(jnp.int32), axis=1)
+    order = jnp.sum(jnp.where(slot[None, :] == columns[:, None], columns[None, :], 0), axis=1)
+    source = place // COLUMNS * COLUMNS + jnp.sum(jnp.where(hit, slot[:, None], 0), axis=0)
+    return jnp.concatenate([order % TILES, order // TILES, source])
+
+
+def split(x):
+    parts = []
+    for _ in range(PARTS - 1):
+        part = x.astype(jnp.bfloat16)
+        parts.append(part)
+        x = x - part.astype(jnp.float32)
+    return (*parts, x.astype(jnp.bfloat16))
+
+
+def band_matrix():
+    shape = (2 * LANES, LANES)
+    row = lax.broadcasted_iota(jnp.int32, shape, 0)
+    source = jnp.where(row < LANES, row, jnp.where(row < LANES + 64, row, row - 2 * LANES))
+    gap = source - lax.broadcasted_iota(jnp.int32, shape, 1)
+    weight = jnp.zeros(shape, jnp.float32)
+    for at, w in ((-2, 1.0), (-1, -8.0), (1, 8.0), (2, -1.0)):
+        weight = jnp.where(gap == at, w, weight)
+    return weight.astype(jnp.bfloat16)
 
 
 def kernel(
     u_hbm, v_hbm, bottom_hbm, scale_ref, mixing_ref, plan_ref, out_ref,
-    ub, vb, bottom, scale, coef, bricks, outbox, rows_out, rows_in, cols_out, cols_in,
+    ub, vb, parts, band, dx, bottom, scale, coef, bricks, outbox, rows_out, rows_in, cols_out, cols_in,
     load_sem, bottom_sem, halo_send, halo_recv, own_sem, send_sem, recv_sem, ready,
 ):
     lon, lat = lax.axis_index("lon"), lax.axis_index("lat")
@@ -51,7 +79,7 @@
     loads = []
     for t in range(TILES):
         cut = pl.ds(t * LANES, LANES)
-        c = pltpu.make_async_copy(bottom_hbm.at[:, cut], bottom.at[t], bottom_sem.at[t])
+        c = pltpu.make_async_copy(bottom_hbm.at[:, :, cut], bottom.at[t], bottom_sem.at[t])
         c.start()
         loads.append(c)
     for g in range(LEV // GROUP):
@@ -60,14 +88,15 @@
             levels = pl.ds(g * GROUP, GROUP)
             for f, (src, dst) in enumerate(((u_hbm, ub), (v_hbm, vb))):
                 c = pltpu.make_async_copy(
-                    src.at[levels, :, cut],
-                    dst.at[levels, t + 1, pl.ds(8, ROWS), :],
+                    src.at[levels, :, :, cut],
+                    dst.at[levels, t, pl.ds(1, ROWS // 8)],
                     load_sem.at[g, t, f],
                 )
                 c.start()
                 loads.append(c)
 
-    scale[...] = jnp.broadcast_to(scale_ref[...], (ROWS, LANES)).T
+    scale[...] = jnp.broadcast_to(scale_ref[...], (ROWS, LANES)).T.reshape(ROWS // 8, 8, LANES)
+    band[...] = band_matrix()
     one = jnp.ones((8, LANES), jnp.float32)
     ratio = None
     for k in range(LEV):
@@ -105,14 +134,16 @@
                 k = g * GROUP + 2 * n + j
                 for t in range(TILES):
                     sea = bottom[t] > k
-                    for buf in (ub, vb):
-                        now = buf[k, t + 1, pl.ds(8, ROWS), :]
-                        buf[k, t + 1, pl.ds(8, ROWS), :] = jnp.where(sea, now, 0.0)
+                    for f, buf in enumerate((ub, vb)):
+                        now = jnp.where(sea, buf[k, t, pl.ds(1, ROWS // 8)], 0.0)
+                        buf[k, t, pl.ds(1, ROWS // 8)] = now
+                        for p, part in enumerate(split(now.reshape(ROWS, LANES))):
+                            parts[f, p, k, t + 1] = part.reshape(ROWS // 16, 16, LANES)
                 for f, buf in enumerate((ub, vb)):
                     at = 4 * k + 2 * f
                     for half in range(2):
-                        first = buf[k, 1, pl.ds(8 + 64 * half, 64), :]
-                        last = buf[k, TILES, pl.ds(8 + 64 * half, 64), :]
+                        first = buf[k, 0, pl.ds(1 + 8 * half, 8)].reshape(64, LANES)
+                        last = buf[k, TILES - 1, pl.ds(1 + 8 * half, 8)].reshape(64, LANES)
                         spot = at + 64 * half
                         here = (lane >= spot) & (lane < spot + 2)
                         west = jnp.where(here, pltpu.roll(first, spot, 1), west)
@@ -120,8 +151,8 @@
             k = g * GROUP + 2 * n
             pair = k // 2
             for t in range(TILES):
-                top = [b[k + j, t + 1, pl.ds(ROWS, 8), :] for j in range(2) for b in (ub, vb)]
-                low = [b[k + j, t + 1, pl.ds(8, 8), :] for j in range(2) for b in (ub, vb)]
+                top = [b[k + j, t, ROWS // 8] for j in range(2) for b in (ub, vb)]
+                low = [b[k + j, t, 1] for j in range(2) for b in (ub, vb)]
                 top = [pltpu.roll(x, s, 0) if s else x for x, s in zip(top, (2, 4, 6, 0))]
                 low = [pltpu.roll(x, s, 0) if s else x for x, s in zip(low, (0, 2, 4, 6))]
                 for side, q in ((0, top), (1, low)):
@@ -179,12 +210,14 @@
         column_copy(side).wait_recv()
 
     def spread_columns(k, _):
-        for f, buf in enumerate((ub, vb)):
+        for f in range(2):
             for half in range(2):
                 spot = 4 * k + 2 * f + 64 * half
-                rows = pl.ds(8 + 64 * half, 64)
-                buf[k, 0, rows, :] = pltpu.roll(cols_in[1], (126 - spot + LANES) % LANES, 1)
-                buf[k, TILES + 1, rows, :] = pltpu.roll(cols_in[0], (LANES - spot) % LANES, 1)
+                west = pltpu.roll(cols_in[1], (126 - spot + LANES) % LANES, 1)
+                east = pltpu.roll(cols_in[0], (LANES - spot) % LANES, 1)
+                for t, x in ((0, west), (TILES + 1, east)):
+                    for n, part in enumerate(split(x)):
+                        parts[f, n, k, t, pl.ds(4 * half, 4)] = part.reshape(4, 16, LANES)
         return _
 
     lax.fori_loop(0, LEV, spread_columns, 0)
@@ -211,48 +244,53 @@
 
     def spread_rows(pair, _):
         for t in range(TILES):
-            for side, shifts, rows in ((0, (6, 4, 2, 0), pl.ds(0, 8)), (1, (0, 6, 4, 2), pl.ds(ROWS + 8, 8))):
+            for side, shifts, rows in ((0, (6, 4, 2, 0), 0), (1, (0, 6, 4, 2), ROWS // 8 + 1)):
                 x = rows_in[side, pair, t]
                 for n, s in enumerate(shifts):
                     buf = (ub, vb)[n % 2]
-                    buf[2 * pair + n // 2, t + 1, rows, :] = pltpu.roll(x, s, 0) if s else x
+                    buf[2 * pair + n // 2, t, rows] = pltpu.roll(x, s, 0) if s else x
         return _
 
     lax.fori_loop(0, LEV // 2, spread_rows, 0)
 
-    lanes = lax.broadcasted_iota(jnp.int32, (8, LANES), 1)
-
-    def slopes(buf, k, c, row):
-        here = buf[k, c + 1, pl.ds(row + 8, 8), :]
-        left = buf[k, c, pl.ds(row + 8, 8), :]
-        right = buf[k, c + 2, pl.ds(row + 8, 8), :]
-
-        def beside(s):
+    nearer = lax.broadcasted_iota(jnp.int32, (LEV * 16, LANES), 1) < 64
+
+    def slope_x(f, c, b):
+        total = None
+        for n in range(PARTS):
+            here, left, right = (parts[f, n, :, c + i, b].reshape(LEV * 16, LANES) for i in (1, 0, 2))
+            cells = jnp.concatenate([here, jnp.where(nearer, right, left)], axis=1)
+            term = jnp.dot(cells, band[...], preferred_element_type=jnp.float32)
+            total = term if total is None else total + term
+        return total.reshape(LEV, 2, 8, LANES)
+
+    def slope_y(buf, k, c, tile):
+        here, near, far = (buf[k, c, tile + i] for i in (1, 0, 2))
+
+        def at(s):
             if s < 0:
-                return pltpu.roll(jnp.where(lanes < LANES + s, here, left), -s, 1)
-            return pltpu.roll(jnp.where(lanes >= s, here, right), LANES - s, 1)
-
-        def above(s):
-            return buf[k, c + 1, pl.ds(row + 8 + s, 8), :]
-
-        def slope(at):
-            return (at(-2) - at(2)) + 8.0 * (at(1) - at(-1))
-
-        return slope(beside), slope(above)
-
-    def compute(j):
-        c = j % TILES
-        row0 = pl.multiple_of(j // TILES * 16, 16)
+                return pltpu.roll(jnp.where(sub < 8 + s, here, near), -s, 0)
+            return pltpu.roll(jnp.where(sub >= s, here, far), 8 - s, 0)
+
+        return (at(-2) - at(2)) + 8.0 * (at(1) - at(-1))
+
+    def slopes(j, slot):
+        for f in range(2):
+            dx[slot, f] = slope_x(f, plan_ref[j], plan_ref[COLUMNS + j])
+
+    def solve(j, slot):
+        c = plan_ref[j]
+        b = plan_ref[COLUMNS + j]
         halves = []
         for h in range(2):
-            row = row0 + 8 * h
-            depth = bottom[c, pl.ds(row, 8), :]
-            wide = scale[pl.ds(row, 8), :]
+            tile = 2 * b + h
+            depth = bottom[c, tile]
+            wide = scale[tile]
             wide4 = 4.0 * wide
             state = []
             for k in range(LEV):
-                ux, uy = slopes(ub, k, c, row)
-                vx, vy = slopes(vb, k, c, row)
+                ux, vx = dx[slot, 0, k, h], dx[slot, 1, k, h]
+                uy, vy = slope_y(ub, k, c, tile), slope_y(vb, k, c, tile)
                 strain = ux * wide - vy
                 okubo = strain * strain + (vx * wide4) * uy
                 value = okubo * jnp.where(depth > k, coef[k], 0.0)
@@ -268,27 +306,33 @@
 
     def send(step):
         to_lon, to_lat = target(lon, lat, step + 1)
-        outbox[step] = bricks[plan_ref[step]]
+        outbox[step] = bricks[plan_ref[2 * COLUMNS + step]]
         pltpu.make_async_remote_copy(
             outbox.at[step], out_ref.at[me], send_sem, recv_sem,
             device_id=(to_lon, to_lat), device_id_type=MESH,
         ).start()
 
-    compute(0)
+    slopes(0, 0)
     pl.semaphore_wait(ready, N_LON - 1)
 
-    def more(j, _):
-        compute(j)
+    def two(n, _):
+        j = 2 * n
+        slopes(j + 1, 1)
+        solve(j, 0)
+        send(j)
+        slopes(lax.rem(j + 2, COLUMNS), 0)
+        solve(j + 1, 1)
+        send(j + 1)
         return _
 
-    lax.fori_loop(1, COLUMNS, more, 0)
+    lax.fori_loop(0, COLUMNS // 2, two, 0)
 
     def rest(step, _):
         send(step)
         return _
 
-    lax.fori_loop(0, DEVICES - 1, rest, 0)
-    out_ref[me] = bricks[plan_ref[DEVICES - 1]]
+    lax.fori_loop(COLUMNS, DEVICES - 1, rest, 0)
+    out_ref[me] = bricks[plan_ref[2 * COLUMNS + DEVICES - 1]]
 
     column_copy(0).wait_send()
     column_copy(1).wait_send()
@@ -304,6 +348,10 @@
     )
     whole.wait_send()
     whole.wait_recv()
+
+
+def by_tile(x):
+    return x.reshape(*x.shape[:-2], x.shape[-2] // 8, 8, x.shape[-1])
 
 
 def body(u_velocity, v_velocity, bottom_level, zonal_scale, mixing, brick_owner):
@@ -320,10 +368,13 @@
         in_specs=[hbm, hbm, hbm, vmem, smem, smem],
         out_specs=vmem,
         scratch_shapes=[
-            pltpu.VMEM((LEV, TILES + 2, ROWS + 16, LANES), jnp.float32),
-            pltpu.VMEM((LEV, TILES + 2, ROWS + 16, LANES), jnp.float32),
-            pltpu.VMEM((TILES, ROWS, LANES), jnp.int32),
-            pltpu.VMEM((ROWS, LANES), jnp.float32),
+            pltpu.VMEM((LEV, TILES, ROWS // 8 + 2, 8, LANES), jnp.float32),
+            pltpu.VMEM((LEV, TILES, ROWS // 8 + 2, 8, LANES), jnp.float32),
+            pltpu.VMEM((2, PARTS, LEV, TILES + 2, ROWS // 16, 16, LANES), jnp.bfloat16),
+            pltpu.VMEM((2 * LANES, LANES), jnp.bfloat16),
+            pltpu.VMEM((2, 2, LEV, 2, 8, LANES), jnp.float32),
+            pltpu.VMEM((TILES, ROWS // 8, 8, LANES), jnp.int32),
+            pltpu.VMEM((ROWS // 8, 8, LANES), jnp.float32),
             pltpu.VMEM((3 * LEV, 8, LANES), jnp.float32),
             pltpu.VMEM(brick, jnp.bfloat16),
             pltpu.VMEM(brick, jnp.bfloat16),
@@ -341,9 +392,9 @@
             pltpu.SemaphoreType.REGULAR,
         ],
         compiler_params=pltpu.CompilerParams(
-            collective_id=0, has_side_effects=True, vmem_limit_bytes=48 << 20
+            collective_id=0, has_side_effects=True, vmem_limit_bytes=56 << 20
         ),
-    )(u_velocity, v_velocity, bottom_level, zonal_scale[None], mixing, plan(brick_owner))
+    )(by_tile(u_velocity), by_tile(v_velocity), by_tile(bottom_level), zonal_scale[None], mixing, plan(brick_owner))
     return out[None]
 
 

time: 61.9 us -> 60.2 us (0.973)
  local copies, waits for them, and re-layouts: 3.58 us -> 1.32 us
  other arithmetic: 0.87 us -> 2.05 us
    unnamed x7 -> x1, local copies, waits for them, and re-layouts: 3.58 us -> 1.32 us
    concatenate x0 -> x1, other arithmetic: none -> 0.64 us  [plan(): return jnp.concatenate([order % TILES, order // TILES, source])]
where the time goes in v2:
time: 60.2 us; the launch traced here: 60.1 us
  Pallas kernels  56.7 us (94%)
  other arithmetic  2.05 us (3%)
  local copies, waits for them, and re-layouts  1.32 us (2%)
    pallas_call x1, Pallas kernels, body(): pl.pallas_call(kernel, out_shape=pltpu.VMEM(brick, jnp.bfloat16), in_spec...  56.7 us
    unnamed x1, local copies, waits for them, and re-layouts  1.32 us

profile of v2, /device:TPU:1, one launch (start us, length us, event | category | flops | bytes accessed | tf_op | source)
XLA Modules:
  0.0 60.1 jit_solution(8359603832397437456)
XLA Ops:
  0.0 0.8 %select_reduce_fusion = s32[128]{0:T(128)S(1)} fusion(s32[128]{0:T(128)} %param.11, s32[128]{0:T(128)S(1)} %fusion.2), kind=kLoop, calls=%fused_computation | loop fusion | flops 49024 | bytes 1536 | tf_op jit(solution)/shard_map/reduce_sum | solution.py:31
  0.9 0.1 select_reduce_fusion.3
  1.0 0.2 convert_reduce_fusion
  1.2 0.1 select_reduce_fusion.1
  1.3 0.1 select_reduce_fusion.2
  1.4 0.6 %pad_add_fusion.plan_ref = s32[192]{0:T(256)} fusion(s32[128]{0:T(128)S(1)} %multiply_add_fusion, s32[32]{0:T(128)S(1)} %get-tuple-element.6, s32[32]{0:T(128)S(1)} %get-tuple-element.5), kind=kLoop, calls=%fused_computation.47 | loop fusion | flops 384 | bytes 1536 | tf_op jit(solution)/shard_map/concatenate | solution.py:39
  2.1 56.7 %shard_map.64 = bf16[128,4,16,128]{3,2,1,0:T(8,128)(2,1)S(1)} custom-call(f32[16,16,8,512]{3,2,1,0:T(8,128)} %bitcast.6, f32[16,16,8,512]{3,2,1,0:T(8,128)} %bitcast.7, s32[16,8,512]{2,1,0:T(8,128)} %bitcast.8, f32[1,128]{1,0:T(1,128)} %bitcast.9, f32[15]{0:T(128)} %mixing_ref.1, s32[192]{0:T(256)} %pad_add_fusion.plan_ref), custom_call_target="tpu_custom_call" | custom-call | tf_op jit(solution)/shard_map/pallas_call | solution.py:365
  58.8 1.3 %copy.8 = bf16[1,128,4,16,128]{4,3,2,1,0:T(8,128)(2,1)} copy(bf16[1,128,4,16,128]{4,3,2,1,0:T(8,128)(2,1)S(1)} %bitcast.5) | data formatting | bytes 4194304
  (4 shorter events, 0.1 us)

commit v3 on v2

--- a/solution.py
+++ b/solution.py
@@ -11,17 +11,16 @@
 DEVICES = N_LON * N_LAT
 COLUMNS = 32
 PARTS = 3
+
 GROUP = 4
 
-
 def target(lon, lat, step):
-    off = (step * 101) % DEVICES
-    x = (lat % 4 // 2 * 2 + lon // 4 + off % 4) % 4
-    y = (lon % 4 + off // 4 % 4) % 4
-    z = (lat // 4 + off // 16 % 4) % 4
-    core = (lat % 2 + off // 64) % 2
-    return x % 2 * 4 + y, z * 4 + x // 2 * 2 + core
-
+    off = (step * 101) & (DEVICES - 1)
+    x = (((lat >> 1 & 1) << 1) + (lon >> 2) + off) & 3
+    y = (lon + (off >> 2)) & 3
+    z = ((lat >> 2) + (off >> 4)) & 3
+    core = (lat + (off >> 6)) & 1
+    return ((x & 1) << 2) + y, (z << 2) + (x >> 1 << 1) + core
 
 def plan(brick_owner):
     lon, lat = lax.axis_index("lon"), lax.axis_index("lat")
@@ -38,7 +37,6 @@
     source = place // COLUMNS * COLUMNS + jnp.sum(jnp.where(hit, slot[:, None], 0), axis=0)
     return jnp.concatenate([order % TILES, order // TILES, source])
 
-
 def split(x):
     parts = []
     for _ in range(PARTS - 1):
@@ -47,21 +45,23 @@
         x = x - part.astype(jnp.float32)
     return (*parts, x.astype(jnp.bfloat16))
 
-
-def band_matrix():
-    shape = (2 * LANES, LANES)
-    row = lax.broadcasted_iota(jnp.int32, shape, 0)
-    source = jnp.where(row < LANES, row, jnp.where(row < LANES + 64, row, row - 2 * LANES))
-    gap = source - lax.broadcasted_iota(jnp.int32, shape, 1)
+def band_matrix(edges):
+    shape = (2 * LANES, 2 * LANES)
+    source = lax.broadcasted_iota(jnp.int32, shape, 0)
+    to = lax.broadcasted_iota(jnp.int32, shape, 1)
+    if edges:
+        same = (source < LANES) == (to < LANES)
+        cell, to = source % LANES, to % LANES
+        source = jnp.where(same, jnp.where(cell < LANES // 2, cell + LANES, cell - LANES), 4 * LANES)
+    gap = source - to
     weight = jnp.zeros(shape, jnp.float32)
     for at, w in ((-2, 1.0), (-1, -8.0), (1, 8.0), (2, -1.0)):
         weight = jnp.where(gap == at, w, weight)
     return weight.astype(jnp.bfloat16)
 
-
 def kernel(
     u_hbm, v_hbm, bottom_hbm, scale_ref, mixing_ref, plan_ref, out_ref,
-    ub, vb, parts, band, dx, bottom, scale, coef, bricks, outbox, rows_out, rows_in, cols_out, cols_in,
+    ub, vb, parts, edges, band, dx, bottom, scale, coef, bricks, outbox, rows_out, rows_in, cols_out, cols_in,
     load_sem, bottom_sem, halo_send, halo_recv, own_sem, send_sem, recv_sem, ready,
 ):
     lon, lat = lax.axis_index("lon"), lax.axis_index("lat")
@@ -96,7 +96,8 @@
                 loads.append(c)
 
     scale[...] = jnp.broadcast_to(scale_ref[...], (ROWS, LANES)).T.reshape(ROWS // 8, 8, LANES)
-    band[...] = band_matrix()
+    band[0] = band_matrix(False)
+    band[1] = band_matrix(True)
     one = jnp.ones((8, LANES), jnp.float32)
     ratio = None
     for k in range(LEV):
@@ -122,6 +123,33 @@
 
     for c in loads[:TILES]:
         c.wait()
+    nearer = lax.broadcasted_iota(jnp.int32, (ROWS, LANES), 1) < 64
+
+    def slopes(g):
+        levels = pl.ds(g * GROUP, GROUP)
+        shape = (GROUP, ROWS // 8, 8, LANES)
+
+        def product(cells, which):
+            total = None
+            for p in range(PARTS):
+                lhs = cells(p).reshape(GROUP * ROWS, 2 * LANES)
+                term = jnp.dot(lhs, band[which], preferred_element_type=jnp.float32)
+                total = term if total is None else total + term
+            return total
+
+        across = product(lambda p: edges[p, levels], 1)
+        for f in range(2):
+            add = across[:, f * LANES : (f + 1) * LANES].reshape(GROUP, ROWS, LANES)
+            for pair in range(2):
+                total = product(lambda p: parts[f, p, pair, levels], 0)
+                for i in range(2):
+                    x = total[:, i * LANES : (i + 1) * LANES].reshape(GROUP, ROWS, LANES)
+                    if pair == 0 and i == 1:
+                        x = x + jnp.where(nearer, 0.0, add)
+                    if pair == 1 and i == 0:
+                        x = x + jnp.where(nearer, add, 0.0)
+                    dx[f, levels, 2 * pair + i] = x.reshape(shape)
+
     west = jnp.zeros((64, LANES), jnp.float32)
     east = jnp.zeros((64, LANES), jnp.float32)
     for g in range(LEV // GROUP):
@@ -132,13 +160,19 @@
             west, east = carry
             for j in range(2):
                 k = g * GROUP + 2 * n + j
-                for t in range(TILES):
-                    sea = bottom[t] > k
-                    for f, buf in enumerate((ub, vb)):
-                        now = jnp.where(sea, buf[k, t, pl.ds(1, ROWS // 8)], 0.0)
+                seas = [bottom[t] > k for t in range(TILES)]
+                for f, buf in enumerate((ub, vb)):
+                    split_tiles = []
+                    for t in range(TILES):
+                        now = jnp.where(seas[t], buf[k, t, pl.ds(1, ROWS // 8)], 0.0)
                         buf[k, t, pl.ds(1, ROWS // 8)] = now
-                        for p, part in enumerate(split(now.reshape(ROWS, LANES))):
-                            parts[f, p, k, t + 1] = part.reshape(ROWS // 16, 16, LANES)
+                        split_tiles.append(split(now.reshape(ROWS, LANES)))
+                        for p in range(PARTS):
+                            parts[f, p, t // 2, k, :, pl.ds(t % 2 * LANES, LANES)] = split_tiles[t][p]
+                    for p in range(PARTS):
+                        edges[p, k, :, pl.ds(f * LANES, LANES)] = jnp.where(
+                            nearer, split_tiles[2][p], split_tiles[1][p]
+                        )
                 for f, buf in enumerate((ub, vb)):
                     at = 4 * k + 2 * f
                     for half in range(2):
@@ -162,6 +196,7 @@
             return west, east
 
         west, east = lax.fori_loop(0, GROUP // 2, mask_pair, (west, east))
+
     cols_out[0] = west
     cols_out[1] = east
 
@@ -206,18 +241,29 @@
     def _():
         rows_in[0] = jnp.zeros(rows_in.shape[1:], jnp.float32)
 
+    for g in range(LEV // GROUP):
+        slopes(g)
+
     for side in range(2):
         column_copy(side).wait_recv()
+
+    even = lane % 2 == 0
+    cells = cols_in[1]
+    cols_in[1] = jnp.where(even, cells - 8.0 * pltpu.roll(cells, LANES - 1, 1), cells)
+    cells = cols_in[0]
+    cols_in[0] = jnp.where(even, -cells, 8.0 * pltpu.roll(cells, 1, 1) - cells)
 
     def spread_columns(k, _):
         for f in range(2):
             for half in range(2):
                 spot = 4 * k + 2 * f + 64 * half
-                west = pltpu.roll(cols_in[1], (126 - spot + LANES) % LANES, 1)
-                east = pltpu.roll(cols_in[0], (LANES - spot) % LANES, 1)
-                for t, x in ((0, west), (TILES + 1, east)):
-                    for n, part in enumerate(split(x)):
-                        parts[f, n, k, t, pl.ds(4 * half, 4)] = part.reshape(4, 16, LANES)
+                west = pltpu.roll(cols_in[1], (LANES - spot) % LANES, 1)
+                east = pltpu.roll(cols_in[0], (126 - spot + LANES) % LANES, 1)
+                west = jnp.where(lane < 2, west, 0.0).reshape(8, 8, LANES)
+                east = jnp.where(lane >= 126, east, 0.0).reshape(8, 8, LANES)
+                tiles = pl.ds(8 * half, 8)
+                dx[f, k, 0, tiles] = dx[f, k, 0, tiles] + west
+                dx[f, k, TILES - 1, tiles] = dx[f, k, TILES - 1, tiles] + east
         return _
 
     lax.fori_loop(0, LEV, spread_columns, 0)
@@ -253,17 +299,6 @@
 
     lax.fori_loop(0, LEV // 2, spread_rows, 0)
 
-    nearer = lax.broadcasted_iota(jnp.int32, (LEV * 16, LANES), 1) < 64
-
-    def slope_x(f, c, b):
-        total = None
-        for n in range(PARTS):
-            here, left, right = (parts[f, n, :, c + i, b].reshape(LEV * 16, LANES) for i in (1, 0, 2))
-            cells = jnp.concatenate([here, jnp.where(nearer, right, left)], axis=1)
-            term = jnp.dot(cells, band[...], preferred_element_type=jnp.float32)
-            total = term if total is None else total + term
-        return total.reshape(LEV, 2, 8, LANES)
-
     def slope_y(buf, k, c, tile):
         here, near, far = (buf[k, c, tile + i] for i in (1, 0, 2))
 
@@ -274,11 +309,7 @@
 
         return (at(-2) - at(2)) + 8.0 * (at(1) - at(-1))
 
-    def slopes(j, slot):
-        for f in range(2):
-            dx[slot, f] = slope_x(f, plan_ref[j], plan_ref[COLUMNS + j])
-
-    def solve(j, slot):
+    def solve(j):
         c = plan_ref[j]
         b = plan_ref[COLUMNS + j]
         halves = []
@@ -289,7 +320,7 @@
             wide4 = 4.0 * wide
             state = []
             for k in range(LEV):
-                ux, vx = dx[slot, 0, k, h], dx[slot, 1, k, h]
+                ux, vx = dx[0, k, c, tile], dx[1, k, c, tile]
                 uy, vy = slope_y(ub, k, c, tile), slope_y(vb, k, c, tile)
                 strain = ux * wide - vy
                 okubo = strain * strain + (vx * wide4) * uy
@@ -312,26 +343,21 @@
             device_id=(to_lon, to_lat), device_id_type=MESH,
         ).start()
 
-    slopes(0, 0)
+    solve(0)
     pl.semaphore_wait(ready, N_LON - 1)
 
-    def two(n, _):
-        j = 2 * n
-        slopes(j + 1, 1)
-        solve(j, 0)
-        send(j)
-        slopes(lax.rem(j + 2, COLUMNS), 0)
-        solve(j + 1, 1)
-        send(j + 1)
+    def both(j, _):
+        send(j - 1)
+        solve(j)
         return _
 
-    lax.fori_loop(0, COLUMNS // 2, two, 0)
+    lax.fori_loop(1, COLUMNS, both, 0)
 
     def rest(step, _):
         send(step)
         return _
 
-    lax.fori_loop(COLUMNS, DEVICES - 1, rest, 0)
+    lax.fori_loop(COLUMNS - 1, DEVICES - 1, rest, 0)
     out_ref[me] = bricks[plan_ref[2 * COLUMNS + DEVICES - 1]]
 
     column_copy(0).wait_send()
@@ -349,10 +375,8 @@
     whole.wait_send()
     whole.wait_recv()
 
-
 def by_tile(x):
     return x.reshape(*x.shape[:-2], x.shape[-2] // 8, 8, x.shape[-1])
-
 
 def body(u_velocity, v_velocity, bottom_level, zonal_scale, mixing, brick_owner):
     brick = (DEVICES, 4, 16, LANES)
@@ -370,9 +394,10 @@
         scratch_shapes=[
             pltpu.VMEM((LEV, TILES, ROWS // 8 + 2, 8, LANES), jnp.float32),
             pltpu.VMEM((LEV, TILES, ROWS // 8 + 2, 8, LANES), jnp.float32),
-            pltpu.VMEM((2, PARTS, LEV, TILES + 2, ROWS // 16, 16, LANES), jnp.bfloat16),
-            pltpu.VMEM((2 * LANES, LANES), jnp.bfloat16),
-            pltpu.VMEM((2, 2, LEV, 2, 8, LANES), jnp.float32),
+            pltpu.VMEM((2, PARTS, TILES // 2, LEV, ROWS, 2 * LANES), jnp.bfloat16),
+            pltpu.VMEM((PARTS, LEV, ROWS, 2 * LANES), jnp.bfloat16),
+            pltpu.VMEM((2, 2 * LANES, 2 * LANES), jnp.bfloat16),
+            pltpu.VMEM((2, LEV, TILES, ROWS // 8, 8, LANES), jnp.float32),
             pltpu.VMEM((TILES, ROWS // 8, 8, LANES), jnp.int32),
             pltpu.VMEM((ROWS // 8, 8, LANES), jnp.float32),
             pltpu.VMEM((3 * LEV, 8, LANES), jnp.float32),
@@ -397,7 +422,6 @@
     )(by_tile(u_velocity), by_tile(v_velocity), by_tile(bottom_level), zonal_scale[None], mixing, plan(brick_owner))
     return out[None]
 
-
 def solution(mesh):
     placed = (P(None, "lat", "lon"), P(None, "lat", "lon"), P("lat", "lon"), P("lat"), P(), P())
     return jax.shard_map(

time: 60.2 us -> 52.3 us (0.87)
  Pallas kernels: 56.7 us -> 48.8 us
    pallas_call x1, Pallas kernels: 56.7 us -> 48.8 us  [body(): pl.pallas_call(kernel, out_shape=pltpu.VMEM(brick, jnp.bfloat16), in_spec...]
where the time goes in v3:
time: 52.3 us; the launch traced here: 52.2 us
  Pallas kernels  48.8 us (93%)
  other arithmetic  2.02 us (4%)
  local copies, waits for them, and re-layouts  1.32 us (3%)
    pallas_call x1, Pallas kernels, body(): pl.pallas_call(kernel, out_shape=pltpu.VMEM(brick, jnp.bfloat16), in_spec...  48.8 us
    unnamed x1, local copies, waits for them, and re-layouts  1.32 us

profile of v3, /device:TPU:1, one launch (start us, length us, event | category | flops | bytes accessed | tf_op | source)
XLA Modules:
  0.0 52.2 jit_solution(4626088723529350250)
XLA Ops:
  0.0 0.8 %select_reduce_fusion = s32[128]{0:T(128)S(1)} fusion(s32[128]{0:T(128)} %param.11, s32[128]{0:T(128)S(1)} %add_add_fusion), kind=kLoop, calls=%fused_computation | loop fusion | flops 49024 | bytes 1536 | tf_op jit(solution)/shard_map/reduce_sum | solution.py:30
  0.9 0.1 select_reduce_fusion.3
  1.0 0.2 convert_reduce_fusion
  1.2 0.1 select_reduce_fusion.1
  1.3 0.1 select_reduce_fusion.2
  1.4 0.6 %pad_add_fusion.plan_ref = s32[192]{0:T(256)} fusion(s32[128]{0:T(128)S(1)} %multiply_add_fusion, s32[32]{0:T(128)S(1)} %get-tuple-element.6, s32[32]{0:T(128)S(1)} %get-tuple-element.5), kind=kLoop, calls=%fused_computation.17 | loop fusion | flops 384 | bytes 1536 | tf_op jit(solution)/shard_map/concatenate | solution.py:38
  2.1 48.8 %shard_map.64 = bf16[128,4,16,128]{3,2,1,0:T(8,128)(2,1)S(1)} custom-call(f32[16,16,8,512]{3,2,1,0:T(8,128)} %bitcast.6, f32[16,16,8,512]{3,2,1,0:T(8,128)} %bitcast.7, s32[16,8,512]{2,1,0:T(8,128)} %bitcast.8, f32[1,128]{1,0:T(1,128)} %bitcast.9, f32[15]{0:T(128)} %mixing_ref.1, s32[192]{0:T(256)} %pad_add_fusion.plan_ref), custom_call_target="tpu_custom_call" | custom-call | tf_op jit(solution)/shard_map/pallas_call | solution.py:389
  50.9 1.3 %copy.8 = bf16[1,128,4,16,128]{4,3,2,1,0:T(8,128)(2,1)} copy(bf16[1,128,4,16,128]{4,3,2,1,0:T(8,128)(2,1)S(1)} %bitcast.5) | data formatting | bytes 4194304
  (4 shorter events, 0.1 us)

commit v4 on v3

--- a/solution.py
+++ b/solution.py
@@ -22,20 +22,29 @@
     core = (lat + (off >> 6)) & 1
     return ((x & 1) << 2) + y, (z << 2) + (x >> 1 << 1) + core
 
-def plan(brick_owner):
-    lon, lat = lax.axis_index("lon"), lax.axis_index("lat")
-    steps = jnp.arange(DEVICES, dtype=jnp.int32)
-    to_lon, to_lat = target(lon, lat, steps + 1)
-    dest = to_lon * N_LAT + to_lat
-    place = jnp.sum(jnp.where(brick_owner[None, :] == dest[:, None], steps[None, :], 0), axis=1)
-    column = place % COLUMNS
-    columns = jnp.arange(COLUMNS, dtype=jnp.int32)
-    hit = column[None, :] == columns[:, None]
-    need = jnp.min(jnp.where(hit, steps[None, :], DEVICES), axis=1)
-    slot = jnp.sum((need[None, :] < need[:, None]).astype(jnp.int32), axis=1)
-    order = jnp.sum(jnp.where(slot[None, :] == columns[:, None], columns[None, :], 0), axis=1)
-    source = place // COLUMNS * COLUMNS + jnp.sum(jnp.where(hit, slot[:, None], 0), axis=0)
-    return jnp.concatenate([order % TILES, order // TILES, source])
+def plan(owner, lon, lat):
+    shape = (DEVICES, DEVICES)
+    down = lax.broadcasted_iota(jnp.int32, shape, 0)
+    along = lax.broadcasted_iota(jnp.int32, shape, 1)
+
+    def total(x, axis):
+        return jnp.broadcast_to(jnp.sum(x.astype(jnp.float32), axis=axis, keepdims=True), shape)
+
+    to_lon, to_lat = target(lon, lat, down + 1)
+    place = total(jnp.where(owner == to_lon * N_LAT + to_lat, along, 0), 1).astype(jnp.int32)
+    place = place & (DEVICES - 1)
+    hit = (place & (COLUMNS - 1)) == along
+    need = jnp.broadcast_to(
+        jnp.min(jnp.where(hit, down, DEVICES).astype(jnp.float32), axis=0, keepdims=True), shape
+    )
+    slot = total(jnp.where(need.T < need, 1, 0), 0)
+    order = total(jnp.where(slot.astype(jnp.int32) == down, jnp.where(along < COLUMNS, along, 0), 0), 1)
+    source = total(jnp.where(hit, slot, 0.0), 1) + (place - (place & (COLUMNS - 1))).astype(jnp.float32)
+    order, source = order.T[:8].astype(jnp.int32), source.T[:8].astype(jnp.int32)
+    order, source = order & (COLUMNS - 1), source & (DEVICES - 1)
+    row = down[:8]
+    return jnp.where(row == 0, order & (TILES - 1), jnp.where(row == 1, order >> 2, source))
+
 
 def split(x):
     parts = []
@@ -60,9 +69,9 @@
     return weight.astype(jnp.bfloat16)
 
 def kernel(
-    u_hbm, v_hbm, bottom_hbm, scale_ref, mixing_ref, plan_ref, out_ref,
+    u_hbm, v_hbm, bottom_hbm, scale_ref, mixing_ref, owner_ref, out_ref,
     ub, vb, parts, edges, band, dx, bottom, scale, coef, bricks, outbox, rows_out, rows_in, cols_out, cols_in,
-    load_sem, bottom_sem, halo_send, halo_recv, own_sem, send_sem, recv_sem, ready,
+    plan_made, plan_ref, plan_sem, load_sem, bottom_sem, halo_send, halo_recv, own_sem, send_sem, recv_sem, ready,
 ):
     lon, lat = lax.axis_index("lon"), lax.axis_index("lat")
     me = lon * N_LAT + lat
@@ -94,6 +103,10 @@
                 )
                 c.start()
                 loads.append(c)
+
+    plan_made[...] = plan(jnp.broadcast_to(owner_ref[...], (DEVICES, DEVICES)), lon, lat)
+    plan_copy = pltpu.make_async_copy(plan_made, plan_ref, plan_sem)
+    plan_copy.start()
 
     scale[...] = jnp.broadcast_to(scale_ref[...], (ROWS, LANES)).T.reshape(ROWS // 8, 8, LANES)
     band[0] = band_matrix(False)
@@ -310,8 +323,8 @@
         return (at(-2) - at(2)) + 8.0 * (at(1) - at(-1))
 
     def solve(j):
-        c = plan_ref[j]
-        b = plan_ref[COLUMNS + j]
+        c = plan_ref[0, j]
+        b = plan_ref[1, j]
         halves = []
         for h in range(2):
             tile = 2 * b + h
@@ -337,12 +350,13 @@
 
     def send(step):
         to_lon, to_lat = target(lon, lat, step + 1)
-        outbox[step] = bricks[plan_ref[2 * COLUMNS + step]]
+        outbox[step] = bricks[plan_ref[2, step]]
         pltpu.make_async_remote_copy(
             outbox.at[step], out_ref.at[me], send_sem, recv_sem,
             device_id=(to_lon, to_lat), device_id_type=MESH,
         ).start()
 
+    plan_copy.wait()
     solve(0)
     pl.semaphore_wait(ready, N_LON - 1)
 
@@ -358,7 +372,7 @@
         return _
 
     lax.fori_loop(COLUMNS - 1, DEVICES - 1, rest, 0)
-    out_ref[me] = bricks[plan_ref[2 * COLUMNS + DEVICES - 1]]
+    out_ref[me] = bricks[plan_ref[2, DEVICES - 1]]
 
     column_copy(0).wait_send()
     column_copy(1).wait_send()
@@ -389,7 +403,7 @@
     out = pl.pallas_call(
         kernel,
         out_shape=pltpu.VMEM(brick, jnp.bfloat16),
-        in_specs=[hbm, hbm, hbm, vmem, smem, smem],
+        in_specs=[hbm, hbm, hbm, vmem, smem, vmem],
         out_specs=vmem,
         scratch_shapes=[
             pltpu.VMEM((LEV, TILES, ROWS // 8 + 2, 8, LANES), jnp.float32),
@@ -407,6 +421,9 @@
             pltpu.VMEM((2, LEV // 2, TILES, 8, LANES), jnp.float32),
             pltpu.VMEM((2, 64, LANES), jnp.float32),
             pltpu.VMEM((2, 64, LANES), jnp.float32),
+            pltpu.VMEM((8, DEVICES), jnp.int32),
+            pltpu.SMEM((8, DEVICES), jnp.int32),
+            dma,
             dma((LEV // GROUP, TILES, 2)),
             dma((TILES,)),
             dma((4,)),
@@ -419,7 +436,7 @@
         compiler_params=pltpu.CompilerParams(
             collective_id=0, has_side_effects=True, vmem_limit_bytes=56 << 20
         ),
-    )(by_tile(u_velocity), by_tile(v_velocity), by_tile(bottom_level), zonal_scale[None], mixing, plan(brick_owner))
+    )(by_tile(u_velocity), by_tile(v_velocity), by_tile(bottom_level), zonal_scale[None], mixing, brick_owner[None])
     return out[None]
 
 def solution(mesh):

time: 52.3 us -> 50.2 us (0.960)
  other arithmetic: 2.02 us -> 0 us
    reduce_sum x4 -> x0, other arithmetic: 1.2 us -> none  [the longest x1 0.82 us: plan(): jnp.sum(jnp.where(brick_owner[None, :] == dest[:, None], steps[None, :],...]
    concatenate x1 -> x0, other arithmetic: 0.64 us -> none  [plan(): return jnp.concatenate([order % TILES, order // TILES, source])]
where the time goes in v4:
time: 50.2 us; the launch traced here: 50.1 us
  Pallas kernels  48.8 us (97%)
  local copies, waits for them, and re-layouts  1.32 us (3%)
    pallas_call x1, Pallas kernels, body(): pl.pallas_call(kernel, out_shape=pltpu.VMEM(brick, jnp.bfloat16), in_spec...  48.8 us
    unnamed x1, local copies, waits for them, and re-layouts  1.32 us

profile of v4, /device:TPU:1, one launch (start us, length us, event | category | flops | bytes accessed | tf_op | source)
XLA Modules:
  0.0 50.1 jit_solution(17289728106753570178)
XLA Ops:
  0.0 48.8 %shard_map.64 = bf16[128,4,16,128]{3,2,1,0:T(8,128)(2,1)S(1)} custom-call(f32[16,16,8,512]{3,2,1,0:T(8,128)} %bitcast.7, f32[16,16,8,512]{3,2,1,0:T(8,128)} %bitcast.8, s32[16,8,512]{2,1,0:T(8,128)} %bitcast.9, f32[1,128]{1,0:T(1,128)} %bitcast.10, f32[15]{0:T(128)} %mixing_ref.1, s32[1,128]{1,0:T(1,128)} %bitcast.11), custom_call_target="tpu_custom_call" | custom-call | tf_op jit(solution)/shard_map/pallas_call | solution.py:403
  48.8 1.3 %copy.8 = bf16[1,128,4,16,128]{4,3,2,1,0:T(8,128)(2,1)} copy(bf16[1,128,4,16,128]{4,3,2,1,0:T(8,128)(2,1)S(1)} %bitcast.6) | data formatting | bytes 4194304

commit v5 on v4

--- a/solution.py
+++ b/solution.py
@@ -79,11 +79,6 @@
 
     def signal(sem, to):
         pl.semaphore_signal(sem, inc=1, device_id=to, device_id_type=MESH)
-
-    for k in range(1, N_LAT):
-        signal(barrier, (lon, (lat + k) % N_LAT))
-    for k in range(1, N_LON):
-        signal(barrier, ((lon + k) % N_LON, lat))
 
     loads = []
     for t in range(TILES):
@@ -103,6 +98,11 @@
                 )
                 c.start()
                 loads.append(c)
+
+    for k in range(1, N_LAT):
+        signal(barrier, (lon, (lat + k) % N_LAT))
+    for k in range(1, N_LON):
+        signal(barrier, ((lon + k) % N_LON, lat))
 
     plan_made[...] = plan(jnp.broadcast_to(owner_ref[...], (DEVICES, DEVICES)), lon, lat)
     plan_copy = pltpu.make_async_copy(plan_made, plan_ref, plan_sem)

time: 50.2 us -> 50 us (level)
  no operation moved by 1% of the time
where the time goes in v5:
time: 50 us; the launch traced here: 49.9 us
  Pallas kernels  48.6 us (97%)
  local copies, waits for them, and re-layouts  1.32 us (3%)
    pallas_call x1, Pallas kernels, body(): pl.pallas_call(kernel, out_shape=pltpu.VMEM(brick, jnp.bfloat16), in_spec...  48.6 us
    unnamed x1, local copies, waits for them, and re-layouts  1.32 us

profile of v5, /device:TPU:1, one launch (start us, length us, event | category | flops | bytes accessed | tf_op | source)
XLA Modules:
  0.0 49.9 jit_solution(2392894107618874354)
XLA Ops:
  0.0 48.6 %shard_map.64 = bf16[128,4,16,128]{3,2,1,0:T(8,128)(2,1)S(1)} custom-call(f32[16,16,8,512]{3,2,1,0:T(8,128)} %bitcast.7, f32[16,16,8,512]{3,2,1,0:T(8,128)} %bitcast.8, s32[16,8,512]{2,1,0:T(8,128)} %bitcast.9, f32[1,128]{1,0:T(1,128)} %bitcast.10, f32[15]{0:T(128)} %mixing_ref.1, s32[1,128]{1,0:T(1,128)} %bitcast.11), custom_call_target="tpu_custom_call" | custom-call | tf_op jit(solution)/shard_map/pallas_call | solution.py:403
  48.6 1.3 %copy.8 = bf16[1,128,4,16,128]{4,3,2,1,0:T(8,128)(2,1)} copy(bf16[1,128,4,16,128]{4,3,2,1,0:T(8,128)(2,1)S(1)} %bitcast.6) | data formatting | bytes 4194304
